TPU v7x, 512 devices: a whole 4x8x8 slice. The times are simulated.
512 devices in a mesh: inst: 16 (over z_lo, x, core), blk: 32 (over y, z_hi).
Axes of the slice: x: 4, y: 8, z: 8 (z_hi: 4, z_lo: 2; z = z_hi * 2 + z_lo), core: 2. Of those that a mesh axis runs over, the one named last changes fastest.
Arguments:
- state: float32 [16, 5, 16, 256, 256], P('inst', None, None, 'blk'), may hold values from -0.53 to 3.9, as said below
- multiples: int32 [7], replicated, may hold values from 1 to 4
Outputs:
- state_change: float32 [16, 5, 16, 256, 256], P('inst', None, None, 'blk')
Inputs may be any that keep to these rules, and one draw needn't show every extreme that they name: `state`: density and pressure lie in 0.7 to 1.3, the axial velocity in 0.2 to 0.8 and the other two velocity components in -0.4 to 0.4; the last variable is the total energy p / 0.4 + rho (u u + v v + w w) / 2.
All inputs are finite; a program needn't handle non-finite values.
Results may differ from a plain program's by a relative error of at most 0.0003.
Values sent between devices are 32-bit elements; how exact they have to be, the bound alone decides.
A program may use at most 64 MiB of HBM per device.

v0:
```python
import math
import jax
import jax.numpy as jnp
from jax import lax
from jax.sharding import PartitionSpec as P

NT = 16
heat_ratio = 1.4
segment_step = 0.05
smooth_weight = 0.5
base_rate = 0.5
diagonal_weight = 3.0


def extended_2(cells, sides, width):
    for axis, dim in sides:
        count = lax.axis_size(axis)
        head = lax.slice_in_dim(cells, 0, width, axis=dim)
        tail = lax.slice_in_dim(cells, cells.shape[dim] - width, cells.shape[dim], axis=dim)
        cells = jnp.concatenate(
            [
                lax.ppermute(tail, axis, [(i, (i + 1) % count) for i in range(count)]),
                cells,
                lax.ppermute(head, axis, [((i + 1) % count, i) for i in range(count)]),
            ],
            axis=dim,
        )
    return cells


def limited(lower, upper):
    return jnp.maximum(0.0, jnp.minimum(lower, upper)) + jnp.minimum(0.0, jnp.maximum(lower, upper))


def take_part(array_in, offset, amount, along):
    return lax.slice_in_dim(array_in, offset, offset + amount, axis=along)


def primitive(conserved):
    density = conserved[:, 0]
    velocity = [conserved[:, 1] / density, conserved[:, 2] / density, conserved[:, 3] / density]
    kinetic = (
        0.5
        * density
        * (velocity[0] * velocity[0] + velocity[1] * velocity[1] + velocity[2] * velocity[2])
    )
    pressure = (heat_ratio - 1.0) * (conserved[:, 4] - kinetic)
    return [density] + velocity + [pressure]


def physical(states, normal):
    density = states[0]
    pressure = states[4]
    velocity = states[1:4]
    normal_speed = velocity[normal]
    energy = pressure / (heat_ratio - 1.0) + 0.5 * density * (
        velocity[0] * velocity[0] + velocity[1] * velocity[1] + velocity[2] * velocity[2]
    )
    conserved = [
        density,
        density * velocity[0],
        density * velocity[1],
        density * velocity[2],
        energy,
    ]
    flux = [density * normal_speed]
    for member in range(3):
        momentum = density * normal_speed * velocity[member]
        if member == normal:
            momentum = momentum + pressure
        flux.append(momentum)
    flux.append((energy + pressure) * normal_speed)
    wave_speed = jnp.abs(normal_speed) + jnp.sqrt(heat_ratio * pressure / density)
    return (flux, conserved, wave_speed)


def divergence(states, along, normal):
    extent = states[0].shape[along]
    interior = extent - 4
    left_side = []
    right_side = []
    for component in states:
        differences = take_part(component, 1, extent - 1, along) - take_part(
            component, 0, extent - 1, along
        )
        slopes = limited(
            take_part(differences, 0, interior + 2, along),
            take_part(differences, 1, interior + 2, along),
        )
        centres = take_part(component, 1, interior + 2, along)
        left_side.append(
            take_part(centres, 0, interior + 1, along)
            + 0.5 * take_part(slopes, 0, interior + 1, along)
        )
        right_side.append(
            take_part(centres, 1, interior + 1, along)
            - 0.5 * take_part(slopes, 1, interior + 1, along)
        )
    left_flux, left_cons, left_speed = physical(left_side, normal)
    right_flux, right_cons, right_speed = physical(right_side, normal)
    wave_speed = jnp.maximum(left_speed, right_speed)
    result = []
    for member in range(5):
        face_flux = 0.5 * (left_flux[member] + right_flux[member]) - 0.5 * wave_speed * (
            right_cons[member] - left_cons[member]
        )
        result.append(
            take_part(face_flux, 1, interior, along) - take_part(face_flux, 0, interior, along)
        )
    return result


def residual(extended):
    states = primitive(extended)
    inner = [component[:, :, 2:-2, :] for component in states]
    circum = divergence(states, 2, 1)
    axial = divergence(
        [jnp.pad(component, ((0, 0), (2, 2), (0, 0), (0, 0)), mode="edge") for component in inner],
        1,
        0,
    )
    radial = divergence(
        [jnp.pad(component, ((0, 0), (0, 0), (0, 0), (2, 2)), mode="edge") for component in inner],
        3,
        2,
    )
    return jnp.stack(
        [axial[member] + circum[member] + radial[member] for member in range(5)], axis=1
    )


def transform_tables(instances):
    indices = jnp.arange(instances, dtype=jnp.int32)
    harmonic = jnp.where(indices < 2, indices * (instances // 2), indices // 2)
    phases = harmonic[:, None] * indices[None, :] % instances
    angles = phases.astype(jnp.float32) * (2.0 * math.pi / instances)
    sine_rows = (indices % 2 == 1) & (indices >= 2)
    basis = jnp.where(sine_rows[:, None], jnp.sin(angles), jnp.cos(angles))
    weights = jnp.where(indices < 2, 1.0 / instances, 2.0 / instances).astype(jnp.float32)
    return (basis * weights[:, None], basis.T)


def pair_solve(right, frequency):
    cosine_part = right[:, 0]
    sine_part = right[:, 1]
    determinant = diagonal_weight * diagonal_weight + frequency * frequency
    return jnp.stack(
        [
            (diagonal_weight * cosine_part - frequency * sine_part) / determinant,
            (diagonal_weight * sine_part + frequency * cosine_part) / determinant,
        ],
        axis=1,
    )


def neighbours(extended):
    circum = extended[:, :, :, :, :-2] + extended[:, :, :, :, 2:]
    middle = extended[:, :, :, :, 1:-1]
    padded = jnp.pad(middle, ((0, 0), (0, 0), (0, 0), (0, 0), (0, 0), (1, 1)))
    return circum + (padded[:, :, :, :, :, :-2] + padded[:, :, :, :, :, 2:])


def body(state, multiples):
    extended = extended_2(state, (("blk", 3),), 4)
    first_sweep = residual(extended)
    segmented = extended[:, :, :, 2:-2] - segment_step * first_sweep
    second_sweep = residual(segmented)
    state_freq, residual_freq = (
        lax.all_to_all(state, "inst", split_axis=2, concat_axis=0, tiled=True),
        lax.all_to_all(second_sweep, "inst", split_axis=2, concat_axis=0, tiled=True),
    )
    forward, inverse = transform_tables(NT)
    layout = residual_freq.shape
    paired = (NT // 2, 2) + layout[1:]
    residual_hat = jnp.dot(
        forward, residual_freq.reshape(NT, -1), precision=lax.Precision.HIGHEST
    ).reshape(paired)
    state_hat = jnp.dot(
        forward, state_freq.reshape(NT, -1), precision=lax.Precision.HIGHEST
    ).reshape(paired)
    frequency = jnp.concatenate(
        [jnp.zeros((1,), jnp.float32), base_rate * multiples.astype(jnp.float32)]
    ).reshape(NT // 2, 1, 1, 1, 1)
    source = jnp.stack([frequency * state_hat[:, 1], -frequency * state_hat[:, 0]], axis=1)
    right_hand = -(residual_hat + source)
    widened = extended_2(right_hand, (("blk", 4),), 3)
    correction = pair_solve(widened, frequency)
    for repeat in range(3):
        trimmed = lax.slice_in_dim(widened, repeat + 1, widened.shape[4] - repeat - 1, axis=4)
        correction = pair_solve(trimmed + smooth_weight * neighbours(correction), frequency)
    change_freq = jnp.dot(
        inverse, correction.reshape(NT, -1), precision=lax.Precision.HIGHEST
    ).reshape(layout)
    return lax.all_to_all(change_freq, "inst", split_axis=0, concat_axis=2, tiled=True)


def solution(mesh):
    return jax.shard_map(
        body,
        mesh=mesh,
        in_specs=(P("inst", None, None, "blk", None), P()),
        out_specs=P("inst", None, None, "blk", None),
        check_vma=False,
    )
```

profile of v0, /device:TPU:25, one launch (start us, length us, event | category | flops | bytes accessed | tf_op | source)
XLA Modules:
  0.0 139.0 jit_solution(2675094903121760378)
XLA Ops:
  0.0 1.5 %fusion.215 = (f32[1,5,16,4,256]{4,3,2,1,0:T(4,128)S(1)}, f32[1,5,16,4,256]{4,3,2,1,0:T(4,128)S(1)}) fusion(f32[1,5,16,8,256]{4,3,2,1,0:T(8,128)} %param.2), kind=kLoop, calls=%fused_computation.532 | loop fusion | bytes 1310720 | tf_op jit(solution)/shard_map/slice | solution.py:19
  1.5 5.8 %collective-permute-start = (f32[1,5,16,4,256]{4,3,2,1,0:T(4,128)S(1)}, f32[1,5,16,4,256]{4,3,2,1,0:T(4,128)S(1)}, u32[]{:S(2)}, u32[]{:S(2)}) collective-permute-start(f32[1,5,16,4,256]{4,3,2,1,0:T(4,128)S(1)} %get-tuple-element.83), channel_id=1, source_target_pairs={{0,1},{1,2},{2,3},{3,4},{4,5},{5,6},{6,7},{7,8},{8,9},{9,10},{10,1... | collective-permute-start | bytes 983048 | tf_op jit(solution)/shard_map/ppermute | solution.py:22
  7.3 6.7 %collective-permute-start.1 = (f32[1,5,16,4,256]{4,3,2,1,0:T(4,128)S(1)}, f32[1,5,16,4,256]{4,3,2,1,0:T(4,128)S(1)}, u32[]{:S(2)}, u32[]{:S(2)}) collective-permute-start(f32[1,5,16,4,256]{4,3,2,1,0:T(4,128)S(1)} %get-tuple-element.84), channel_id=1, source_target_pairs={{1,0},{2,1},{3,2},{4,3},{5,4},{6,5},{7,6},{8,7},{9,8},{10,9},{11,1... | collective-permute-start | bytes 983048 | tf_op jit(solution)/shard_map/ppermute | solution.py:24
  14.0 0.9 copy.86
  14.9 6.2 %all-to-all-start.1 = ((f32[1,5,16,8,256]{4,3,1,0,2:T(8,128)}), f32[1,5,16,8,256]{4,3,1,0,2:T(8,128)S(1)}, u32[]{:S(2)}, u32[]{:S(2)}) async-start(f32[1,5,16,8,256]{4,3,1,0,2:T(8,128)} %copy.86), calls=%async_computation.1 | async-start | bytes 1310720 | tf_op jit(solution)/shard_map/all_to_all | solution.py:169
  21.0 3.3 %collective-permute-done = f32[1,5,16,4,256]{4,3,2,1,0:T(4,128)S(1)} collective-permute-done((f32[1,5,16,4,256]{4,3,2,1,0:T(4,128)S(1)}, f32[1,5,16,4,256]{4,3,2,1,0:T(4,128)S(1)}, u32[]{:S(2)}, u32[]{:S(2)}) %collective-permute-start) | collective-permute-done | bytes 327712 | tf_op jit(solution)/shard_map/ppermute | solution.py:22
  24.3 5.7 %collective-permute-done.1 = f32[1,5,16,4,256]{4,3,2,1,0:T(4,128)S(1)} collective-permute-done((f32[1,5,16,4,256]{4,3,2,1,0:T(4,128)S(1)}, f32[1,5,16,4,256]{4,3,2,1,0:T(4,128)S(1)}, u32[]{:S(2)}, u32[]{:S(2)}) %collective-permute-start.1) | collective-permute-done | bytes 327712 | tf_op jit(solution)/shard_map/ppermute | solution.py:24
  31.4 0.7 multiply_subtract_fusion.5
  32.0 0.4 multiply_subtract_fusion.6
  32.5 0.4 multiply_subtract_fusion.7
  37.5 1.4 multiply_subtract_fusion
  38.9 0.8 multiply_subtract_fusion.2
  39.7 0.8 multiply_subtract_fusion.3
  40.5 0.4 multiply_subtract_fusion.8
  41.1 0.7 multiply_subtract_fusion.1
  42.1 0.9 multiply_subtract_fusion.15
  43.0 0.8 multiply_subtract_fusion.16
  44.5 0.4 slice_subtract_fusion
  45.6 0.7 fusion.220
  46.8 1.0 multiply_subtract_fusion.25
  47.8 0.9 multiply_subtract_fusion.27
  48.7 0.9 multiply_subtract_fusion.28
  49.6 0.7 slice_subtract_fusion.11
  50.4 0.7 slice_subtract_fusion.12
  51.1 0.7 slice_subtract_fusion.13
  51.9 0.7 slice_subtract_fusion.14
  52.6 0.7 slice_subtract_fusion.15
  53.8 0.5 copy-done.22
  54.4 0.6 copy-done.24
  55.2 0.8 minimum_add_fusion.24
  56.5 0.5 copy-done.26
  57.1 0.6 copy-done.28
  58.0 0.8 minimum_add_fusion.23
  60.2 0.6 copy-done.20
  61.2 1.6 %copy.101 = f32[1,16,8,1]{2,1,0,3:T(8,128)} copy(f32[1,16,8,1]{3,2,1,0:T(8,128)} %get-tuple-element.103) | data formatting | bytes 1024 | tf_op jit(solution)/shard_map/jit(_pad)/slice | solution.py:123
  62.8 1.6 %copy.102 = f32[1,16,8,1]{2,1,0,3:T(8,128)} copy(f32[1,16,8,1]{3,2,1,0:T(8,128)} %get-tuple-element.104) | data formatting | bytes 1024 | tf_op jit(solution)/shard_map/jit(_pad)/slice | solution.py:123
  64.4 0.8 reshape.866
  65.3 0.8 reshape.867
  66.5 0.8 multiply_subtract_fusion.20
  67.3 0.5 multiply_subtract_fusion.23
  67.8 0.4 multiply_subtract_fusion.21
  68.2 0.5 copy-done.5
  69.0 0.7 copy-done.2
  69.9 0.9 multiply_subtract_fusion.10
  70.8 0.5 multiply_subtract_fusion.11
  71.3 0.3 copy-done.19
  71.9 0.5 multiply_subtract_fusion.22
  72.4 0.4 copy-done.17
  73.4 0.6 copy-done.16
  74.1 0.9 copy.84
  75.0 7.0 %all-to-all-start = ((f32[1,5,16,8,256]{4,3,1,0,2:T(8,128)}), f32[1,5,16,8,256]{4,3,1,0,2:T(8,128)S(1)}, u32[]{:S(2)}, u32[]{:S(2)}) async-start(f32[1,5,16,8,256]{4,3,1,0,2:T(8,128)} %copy.84), calls=%async_computation | async-start | bytes 1310720 | tf_op jit(solution)/shard_map/all_to_all | solution.py:170
  82.4 0.9 convolution_bitcast_fusion.1
  83.5 9.7 %all-to-all-done = f32[1,5,16,8,256]{4,3,1,0,2:T(8,128)S(1)} async-done(((f32[1,5,16,8,256]{4,3,1,0,2:T(8,128)}), f32[1,5,16,8,256]{4,3,1,0,2:T(8,128)S(1)}, u32[]{:S(2)}, u32[]{:S(2)}) %all-to-all-start) | async-done | bytes 655392 | tf_op jit(solution)/shard_map/all_to_all | solution.py:170
  93.5 0.9 fusion.2
  94.5 4.2 %collective-permute-start.2 = (f32[8,2,5,1,3,256]{5,0,4,2,1,3:T(8,128)S(1)}, f32[8,2,5,1,3,256]{5,0,4,2,1,3:T(8,128)S(1)}, u32[]{:S(2)}, u32[]{:S(2)}) collective-permute-start(f32[8,2,5,1,3,256]{5,0,4,2,1,3:T(8,128)S(1)} %get-tuple-element.81), channel_id=1, source_target_pairs={{0,1},{1,2},{2,3},{3,4},{4,5},{5,6},{6,7},{7,8},{8,9},{9,10},{10,1... | collective-permute-start | bytes 737288 | tf_op jit(solution)/shard_map/ppermute | solution.py:22
  98.7 4.0 %collective-permute-start.3 = (f32[8,2,5,1,3,256]{5,0,4,2,1,3:T(8,128)S(1)}, f32[8,2,5,1,3,256]{5,0,4,2,1,3:T(8,128)S(1)}, u32[]{:S(2)}, u32[]{:S(2)}) collective-permute-start(f32[8,2,5,1,3,256]{5,0,4,2,1,3:T(8,128)S(1)} %get-tuple-element.82), channel_id=1, source_target_pairs={{1,0},{2,1},{3,2},{4,3},{5,4},{6,5},{7,6},{8,7},{9,8},{10,9},{11,1... | collective-permute-start | bytes 737288 | tf_op jit(solution)/shard_map/ppermute | solution.py:24
  102.8 6.5 %collective-permute-done.2 = f32[8,2,5,1,3,256]{5,0,4,2,1,3:T(8,128)S(1)} collective-permute-done((f32[8,2,5,1,3,256]{5,0,4,2,1,3:T(8,128)S(1)}, f32[8,2,5,1,3,256]{5,0,4,2,1,3:T(8,128)S(1)}, u32[]{:S(2)}, u32[]{:S(2)}) %collective-permute-start.2) | collective-permute-done | bytes 245792 | tf_op jit(solution)/shard_map/ppermute | solution.py:22
  109.3 8.0 %collective-permute-done.3 = f32[8,2,5,1,3,256]{5,0,4,2,1,3:T(8,128)S(1)} collective-permute-done((f32[8,2,5,1,3,256]{5,0,4,2,1,3:T(8,128)S(1)}, f32[8,2,5,1,3,256]{5,0,4,2,1,3:T(8,128)S(1)}, u32[]{:S(2)}, u32[]{:S(2)}) %collective-permute-start.3) | collective-permute-done | bytes 245792 | tf_op jit(solution)/shard_map/ppermute | solution.py:24
  117.6 0.4 select_maximum_fusion
  118.6 0.4 select_maximum_fusion.1
  120.9 0.8 convolution_bitcast_fusion
  121.7 0.4 copy.91
  122.1 16.0 %all_to_all.48 = f32[16,5,1,8,256]{4,3,1,2,0:T(8,128)S(1)} all-to-all(f32[16,5,1,8,256]{4,3,1,2,0:T(8,128)S(1)} %copy.91), channel_id=1, replica_groups=mesh['inst'=16,'blk'=32] {'inst'}, dimensions={0} | all-to-all | bytes 1310720 | tf_op jit(solution)/shard_map/all_to_all | solution.py:194
  138.1 0.9 copy.92
  (243 shorter events, 16.2 us)
Async XLA Ops:
  0.0 14.0 %copy-start = (f32[1,5,16,8,256]{4,3,2,1,0:T(8,128)S(1)}, f32[1,5,16,8,256]{4,3,2,1,0:T(8,128)}, u32[]{:S(2)}) copy-start(f32[1,5,16,8,256]{4,3,2,1,0:T(8,128)} %param.2) | copy-start | bytes 1966084
  1.5 22.8 %collective-permute-start = (f32[1,5,16,4,256]{4,3,2,1,0:T(4,128)S(1)}, f32[1,5,16,4,256]{4,3,2,1,0:T(4,128)S(1)}, u32[]{:S(2)}, u32[]{:S(2)}) collective-permute-start(f32[1,5,16,4,256]{4,3,2,1,0:T(4,128)S(1)} %get-tuple-element.83), channel_id=1, source_target_pairs={{0,1},{1,2},{2,3},{3,4},{4,5},{5,6},{6,7},{7,8},{8,9},{9,10},{10,1... | collective-permute-start | bytes 983048 | tf_op jit(solution)/shard_map/ppermute | solution.py:22
  7.3 22.7 %collective-permute-start.1 = (f32[1,5,16,4,256]{4,3,2,1,0:T(4,128)S(1)}, f32[1,5,16,4,256]{4,3,2,1,0:T(4,128)S(1)}, u32[]{:S(2)}, u32[]{:S(2)}) collective-permute-start(f32[1,5,16,4,256]{4,3,2,1,0:T(4,128)S(1)} %get-tuple-element.84), channel_id=1, source_target_pairs={{1,0},{2,1},{3,2},{4,3},{5,4},{6,5},{7,6},{8,7},{9,8},{10,9},{11,1... | collective-permute-start | bytes 983048 | tf_op jit(solution)/shard_map/ppermute | solution.py:24
  14.9 60.2 %all-to-all-start.1 = ((f32[1,5,16,8,256]{4,3,1,0,2:T(8,128)}), f32[1,5,16,8,256]{4,3,1,0,2:T(8,128)S(1)}, u32[]{:S(2)}, u32[]{:S(2)}) async-start(f32[1,5,16,8,256]{4,3,1,0,2:T(8,128)} %copy.86), calls=%async_computation.1 | async-start | bytes 1310720 | tf_op jit(solution)/shard_map/all_to_all | solution.py:169
  46.6 1.2 copy-start.30
  47.8 1.8 %copy-start.6 = (f32[1,17,8,256]{3,2,1,0:T(8,128)}, f32[1,17,8,256]{3,2,1,0:T(8,128)S(1)}, u32[]{:S(2)}) copy-start(f32[1,17,8,256]{3,2,1,0:T(8,128)S(1)} %get-tuple-element.18) | copy-start | bytes 417796
  47.8 1.8 %copy-start.8 = (f32[1,17,8,256]{3,2,1,0:T(8,128)}, f32[1,17,8,256]{3,2,1,0:T(8,128)S(1)}, u32[]{:S(2)}) copy-start(f32[1,17,8,256]{3,2,1,0:T(8,128)S(1)} %get-tuple-element.19) | copy-start | bytes 417796
  47.8 1.8 %copy-start.10 = (f32[1,17,8,256]{3,2,1,0:T(8,128)}, f32[1,17,8,256]{3,2,1,0:T(8,128)S(1)}, u32[]{:S(2)}) copy-start(f32[1,17,8,256]{3,2,1,0:T(8,128)S(1)} %get-tuple-element.20) | copy-start | bytes 417796
  47.8 1.8 %copy-start.12 = (f32[1,17,8,256]{3,2,1,0:T(8,128)}, f32[1,17,8,256]{3,2,1,0:T(8,128)S(1)}, u32[]{:S(2)}) copy-start(f32[1,17,8,256]{3,2,1,0:T(8,128)S(1)} %get-tuple-element.21) | copy-start | bytes 417796
  53.7 0.6 copy-start.22
  54.3 0.6 copy-start.24
  56.4 0.6 copy-start.26
  57.1 0.6 copy-start.28
  60.2 0.6 copy-start.20
  64.4 2.1 %copy-start.14 = (f32[1,16,8,258]{3,2,1,0:T(8,128)S(1)}, f32[1,16,8,258]{3,2,1,0:T(8,128)}, u32[]{:S(2)}) copy-start(f32[1,16,8,258]{3,2,1,0:T(8,128)} %minimum_add_fusion.24) | copy-start | bytes 396292
  64.4 2.1 %copy-start.15 = (f32[1,16,8,258]{3,2,1,0:T(8,128)S(1)}, f32[1,16,8,258]{3,2,1,0:T(8,128)}, u32[]{:S(2)}) copy-start(f32[1,16,8,258]{3,2,1,0:T(8,128)} %minimum_add_fusion.23) | copy-start | bytes 396292
  64.4 2.1 %copy-start.21 = (f32[1,16,8,2]{3,2,1,0:T(8,128)S(1)}, f32[1,16,8,2]{3,2,1,0:T(8,128)}, u32[]{:S(2)}) copy-start(f32[1,16,8,2]{3,2,1,0:T(8,128)} %copy-done.20) | copy-start | bytes 3076
  64.4 2.1 %copy-start.23 = (f32[1,16,8,2]{3,2,1,0:T(8,128)S(1)}, f32[1,16,8,2]{3,2,1,0:T(8,128)}, u32[]{:S(2)}) copy-start(f32[1,16,8,2]{3,2,1,0:T(8,128)} %copy-done.22) | copy-start | bytes 3076
  64.4 2.1 %copy-start.25 = (f32[1,16,8,2]{3,2,1,0:T(8,128)S(1)}, f32[1,16,8,2]{3,2,1,0:T(8,128)}, u32[]{:S(2)}) copy-start(f32[1,16,8,2]{3,2,1,0:T(8,128)} %copy-done.24) | copy-start | bytes 3076
  64.4 2.1 %copy-start.27 = (f32[1,16,8,2]{3,2,1,0:T(8,128)S(1)}, f32[1,16,8,2]{3,2,1,0:T(8,128)}, u32[]{:S(2)}) copy-start(f32[1,16,8,2]{3,2,1,0:T(8,128)} %copy-done.26) | copy-start | bytes 3076
  64.4 2.1 %copy-start.29 = (f32[1,16,8,2]{3,2,1,0:T(8,128)S(1)}, f32[1,16,8,2]{3,2,1,0:T(8,128)}, u32[]{:S(2)}) copy-start(f32[1,16,8,2]{3,2,1,0:T(8,128)} %copy-done.28) | copy-start | bytes 3076
  67.8 1.0 copy-start.5
  67.8 1.0 copy-start.4
  67.8 1.1 copy-start.3
  68.7 1.0 copy-start.2
  68.8 1.0 copy-start.1
  70.8 0.9 copy-start.19
  70.8 1.0 copy-start.18
  71.9 0.9 copy-start.17
  71.9 1.0 copy-start.7
  71.9 1.0 copy-start.9
  71.9 1.1 copy-start.11
  71.9 1.1 copy-start.13
  71.9 1.1 copy-start.31
  73.1 0.9 copy-start.16
  74.1 7.9 %copy-start.32 = (s32[7]{0:T(128)S(1)}, s32[7]{0:T(128)}, u32[]{:S(2)}) copy-start(s32[7]{0:T(128)} %param.3) | copy-start | bytes 88
  75.0 18.2 %all-to-all-start = ((f32[1,5,16,8,256]{4,3,1,0,2:T(8,128)}), f32[1,5,16,8,256]{4,3,1,0,2:T(8,128)S(1)}, u32[]{:S(2)}, u32[]{:S(2)}) async-start(f32[1,5,16,8,256]{4,3,1,0,2:T(8,128)} %copy.84), calls=%async_computation | async-start | bytes 1310720 | tf_op jit(solution)/shard_map/all_to_all | solution.py:170
  94.5 14.8 %collective-permute-start.2 = (f32[8,2,5,1,3,256]{5,0,4,2,1,3:T(8,128)S(1)}, f32[8,2,5,1,3,256]{5,0,4,2,1,3:T(8,128)S(1)}, u32[]{:S(2)}, u32[]{:S(2)}) collective-permute-start(f32[8,2,5,1,3,256]{5,0,4,2,1,3:T(8,128)S(1)} %get-tuple-element.81), channel_id=1, source_target_pairs={{0,1},{1,2},{2,3},{3,4},{4,5},{5,6},{6,7},{7,8},{8,9},{9,10},{10,1... | collective-permute-start | bytes 737288 | tf_op jit(solution)/shard_map/ppermute | solution.py:22
  98.7 18.5 %collective-permute-start.3 = (f32[8,2,5,1,3,256]{5,0,4,2,1,3:T(8,128)S(1)}, f32[8,2,5,1,3,256]{5,0,4,2,1,3:T(8,128)S(1)}, u32[]{:S(2)}, u32[]{:S(2)}) collective-permute-start(f32[8,2,5,1,3,256]{5,0,4,2,1,3:T(8,128)S(1)} %get-tuple-element.82), channel_id=1, source_target_pairs={{1,0},{2,1},{3,2},{4,3},{5,4},{6,5},{7,6},{8,7},{9,8},{10,9},{11,1... | collective-permute-start | bytes 737288 | tf_op jit(solution)/shard_map/ppermute | solution.py:24
where the time goes:
time: 140 us; the launch traced here: 139 us
  starting transfers between devices  33.9 us (24%)
  waiting for transfers between devices  33.1 us (24%)
  other arithmetic  30.4 us (22%)
  local copies, waits for them, and re-layouts  21.4 us (15%)
  blocking collectives  16 us (11%)
  matrix products  2.59 us (2%)
  between operations  1.65 us (1%)
    all_to_all x1, blocking collectives, body(): lax.all_to_all(change_freq, 'inst', split_axis=0, concat_axis=2, tiled=True)  16 us
    sub x20, other arithmetic, divergence(): 0.5 * (left_flux[member] + right_flux[member])  13.7 us
    ppermute x2, waiting for transfers between devices, extended_2(): lax.ppermute(head, axis, [((i + 1) % count, i) for i in range(count)])  13.7 us
    ppermute x2, starting transfers between devices, extended_2(): lax.ppermute(head, axis, [((i + 1) % count, i) for i in range(count)])  10.7 us
    ppermute x2, starting transfers between devices, extended_2(): lax.ppermute(tail, axis, [(i, (i + 1) % count) for i in range(count)])  10.1 us
    ppermute x2, waiting for transfers between devices, extended_2(): lax.ppermute(tail, axis, [(i, (i + 1) % count) for i in range(count)])  9.72 us
    all_to_all x1, waiting for transfers between devices, body(): lax.all_to_all(second_sweep, 'inst', split_axis=2, concat_axis=0, tiled=T...  9.7 us
    unnamed x70, local copies, waits for them, and re-layouts  7.32 us
  transfers between devices with their start and end apart: 6, of which 5 were waited for; matrix products, arithmetic and copies ran while one was open for 29% of the time, Pallas kernels for 0%

commit v1 on v0

--- a/solution.py
+++ b/solution.py
@@ -10,6 +10,12 @@
 smooth_weight = 0.5
 base_rate = 0.5
 diagonal_weight = 3.0
+
+
+def swap_blocks(array, axis, split, join):
+    parts = jnp.split(array, lax.axis_size(axis), axis=split)
+    incoming = lax.all_to_all(jnp.stack(parts), axis, 0, 0)
+    return jnp.concatenate(incoming, axis=join)
 
 
 def extended_2(cells, sides, width):
@@ -166,7 +172,7 @@
     segmented = extended[:, :, :, 2:-2] - segment_step * first_sweep
     second_sweep = residual(segmented)
     state_freq, residual_freq = (
-        lax.all_to_all(state, "inst", split_axis=2, concat_axis=0, tiled=True),
+        swap_blocks(state, "inst", 2, 0),
         lax.all_to_all(second_sweep, "inst", split_axis=2, concat_axis=0, tiled=True),
     )
     forward, inverse = transform_tables(NT)

time: 140 us -> 139 us (level)
  waiting for transfers between devices: 33.1 us -> 23.8 us
  local copies, waits for them, and re-layouts: 21.4 us -> 30.1 us
    unnamed x70 -> x83, local copies, waits for them, and re-layouts: 7.32 us -> 15.5 us
    ppermute x2, waiting for transfers between devices: 13.7 us -> 7.15 us  [extended_2(): lax.ppermute(head, axis, [((i + 1) % count, i) for i in range(count)])]
    ppermute x2, waiting for transfers between devices: 9.72 us -> 6.65 us  [extended_2(): lax.ppermute(tail, axis, [(i, (i + 1) % count) for i in range(count)])]
  transfers between devices with their start and end apart: 6 -> 6, of which waited for: 5 -> 3; matrix products, arithmetic and copies ran while one was open for 29% -> 35% of each run, Pallas kernels for 0% -> 0%
where the time goes in v1:
time: 139 us
  starting transfers between devices  33.7 us (24%)
  other arithmetic  30.4 us (22%)
  local copies, waits for them, and re-layouts  30.1 us (22%)
  waiting for transfers between devices  23.8 us (17%)
  blocking collectives  16.3 us (12%)
  matrix products  2.59 us (2%)
  between operations  1.66 us (1%)
    all_to_all x1, blocking collectives, body(): lax.all_to_all(change_freq, 'inst', split_axis=0, concat_axis=2, tiled=True)  16.3 us
    unnamed x83, local copies, waits for them, and re-layouts  15.5 us
    sub x20, other arithmetic, divergence(): 0.5 * (left_flux[member] + right_flux[member])  13.7 us
    ppermute x2, starting transfers between devices, extended_2(): lax.ppermute(head, axis, [((i + 1) % count, i) for i in range(count)])  11.4 us
    all_to_all x1, waiting for transfers between devices, body(): lax.all_to_all(second_sweep, 'inst', split_axis=2, concat_axis=0, tiled=T...  10 us
    ppermute x2, starting transfers between devices, extended_2(): lax.ppermute(tail, axis, [(i, (i + 1) % count) for i in range(count)])  9.4 us
    ppermute x2, waiting for transfers between devices, extended_2(): lax.ppermute(head, axis, [((i + 1) % count, i) for i in range(count)])  7.15 us
    all_to_all x1, starting transfers between devices, body(): lax.all_to_all(second_sweep, 'inst', split_axis=2, concat_axis=0, tiled=T...  6.75 us
  transfers between devices with their start and end apart: 6, of which 3 were waited for; matrix products, arithmetic and copies ran while one was open for 35% of the time, Pallas kernels for 0%

profile of v1, /device:TPU:25, one launch (start us, length us, event | category | flops | bytes accessed | tf_op | source)
XLA Modules:
  0.0 138.5 jit_solution(3278713283901938562)
XLA Ops:
  0.0 1.5 %fusion.215 = (f32[1,5,16,4,256]{4,3,2,1,0:T(4,128)S(1)}, f32[1,5,16,4,256]{4,3,2,1,0:T(4,128)S(1)}) fusion(f32[1,5,16,8,256]{4,3,2,1,0:T(8,128)} %param.2), kind=kLoop, calls=%fused_computation.548 | loop fusion | bytes 1310720 | tf_op jit(solution)/shard_map/slice | solution.py:25
  1.5 5.8 %collective-permute-start = (f32[1,5,16,4,256]{4,3,2,1,0:T(4,128)S(1)}, f32[1,5,16,4,256]{4,3,2,1,0:T(4,128)S(1)}, u32[]{:S(2)}, u32[]{:S(2)}) collective-permute-start(f32[1,5,16,4,256]{4,3,2,1,0:T(4,128)S(1)} %get-tuple-element.83), channel_id=1, source_target_pairs={{0,1},{1,2},{2,3},{3,4},{4,5},{5,6},{6,7},{7,8},{8,9},{9,10},{10,1... | collective-permute-start | bytes 983048 | tf_op jit(solution)/shard_map/ppermute | solution.py:28
  7.3 6.7 %collective-permute-start.1 = (f32[1,5,16,4,256]{4,3,2,1,0:T(4,128)S(1)}, f32[1,5,16,4,256]{4,3,2,1,0:T(4,128)S(1)}, u32[]{:S(2)}, u32[]{:S(2)}) collective-permute-start(f32[1,5,16,4,256]{4,3,2,1,0:T(4,128)S(1)} %get-tuple-element.84), channel_id=1, source_target_pairs={{1,0},{2,1},{3,2},{4,3},{5,4},{6,5},{7,6},{8,7},{9,8},{10,9},{11,1... | collective-permute-start | bytes 983048 | tf_op jit(solution)/shard_map/ppermute | solution.py:30
  14.0 0.6 constant_dynamic-update-slice_fusion.15
  14.6 0.6 constant_dynamic-update-slice_fusion.14
  15.2 0.6 constant_dynamic-update-slice_fusion.13
  15.8 0.6 constant_dynamic-update-slice_fusion.12
  16.5 0.6 constant_dynamic-update-slice_fusion.11
  17.1 0.6 constant_dynamic-update-slice_fusion.10
  17.7 0.6 constant_dynamic-update-slice_fusion.9
  18.3 0.6 constant_dynamic-update-slice_fusion.8
  18.9 0.6 constant_dynamic-update-slice_fusion.7
  19.6 0.6 constant_dynamic-update-slice_fusion.6
  20.2 0.6 constant_dynamic-update-slice_fusion.5
  20.8 0.6 constant_dynamic-update-slice_fusion.4
  21.4 0.6 constant_dynamic-update-slice_fusion.3
  22.0 0.6 constant_dynamic-update-slice_fusion.2
  22.7 0.6 constant_dynamic-update-slice_fusion.1
  23.3 0.6 constant_dynamic-update-slice_fusion
  23.9 6.2 %all-to-all-start.1 = ((f32[16,1,5,1,8,256]{5,4,2,3,1,0:T(8,128)}), f32[16,1,5,1,8,256]{5,4,2,3,1,0:T(8,128)S(1)}, u32[]{:S(2)}, u32[]{:S(2)}) async-start(f32[16,1,5,1,8,256]{5,4,2,3,1,0:T(8,128)} %constant_dynamic-update-slice_fusion), calls=%async_computation.1 | async-start | bytes 1310720 | tf_op jit(solution)/shard_map/all_to_all | solution.py:17
  31.5 0.7 multiply_subtract_fusion.5
  37.6 1.4 %multiply_subtract_fusion = (f32[1,16,12,257]{3,2,1,0:T(8,128)S(1)}, f32[1,16,12,257]{3,2,1,0:T(8,128)S(1)}, f32[1,16,12,257]{3,2,1,0:T(8,128)S(1)}, f32[1,16,12,257]{3,2,1,0:T(8,128)S(1)}, f32[1,16,12,257]{3,2,1,0:T(8,128)S(1)}) fusion(f32[1,16,12,258]{3,2,1,0:T(8,128)S(1)} %minimum_add_fusion.1, f32[1,16,12,256]{3,2,1,0:T(8,128)S(1)} %slice.1878, ...), kind=kLoop, calls=%fused_computation.105 | loop fusion | flops 3306048 | bytes 3959040 | tf_op jit(solution)/shard_map/sub | solution.py:110
  39.0 0.8 multiply_subtract_fusion.2
  39.8 0.8 multiply_subtract_fusion.3
  41.2 0.7 multiply_subtract_fusion.1
  42.3 0.9 multiply_subtract_fusion.15
  43.2 0.8 multiply_subtract_fusion.16
  45.8 0.7 fusion.220
  47.0 1.0 multiply_subtract_fusion.25
  48.0 0.9 multiply_subtract_fusion.27
  48.8 0.9 multiply_subtract_fusion.28
  49.8 0.7 slice_subtract_fusion.11
  50.5 0.7 slice_subtract_fusion.12
  51.3 0.7 slice_subtract_fusion.13
  52.0 0.7 slice_subtract_fusion.14
  52.7 0.7 slice_subtract_fusion.15
  53.9 0.5 copy-done.22
  54.5 0.6 copy-done.24
  55.4 0.8 minimum_add_fusion.24
  56.7 0.5 copy-done.26
  57.2 0.6 copy-done.28
  58.1 0.8 minimum_add_fusion.23
  60.3 0.6 copy-done.20
  61.3 1.6 %copy.158 = f32[1,16,8,1]{2,1,0,3:T(8,128)} copy(f32[1,16,8,1]{3,2,1,0:T(8,128)} %get-tuple-element.103) | data formatting | bytes 1024 | tf_op jit(solution)/shard_map/jit(_pad)/slice | solution.py:129
  62.9 1.6 %copy.159 = f32[1,16,8,1]{2,1,0,3:T(8,128)} copy(f32[1,16,8,1]{3,2,1,0:T(8,128)} %get-tuple-element.104) | data formatting | bytes 1024 | tf_op jit(solution)/shard_map/jit(_pad)/slice | solution.py:129
  64.6 0.8 reshape.862
  65.4 0.8 reshape.863
  66.7 0.8 multiply_subtract_fusion.20
  69.1 0.7 copy-done.2
  70.0 0.9 multiply_subtract_fusion.10
  70.9 0.5 multiply_subtract_fusion.11
  73.6 0.6 copy-done.16
  74.2 0.9 copy.127
  75.2 6.7 %all-to-all-start = ((f32[1,5,16,8,256]{4,3,1,0,2:T(8,128)}), f32[1,5,16,8,256]{4,3,1,0,2:T(8,128)S(1)}, u32[]{:S(2)}, u32[]{:S(2)}) async-start(f32[1,5,16,8,256]{4,3,1,0,2:T(8,128)} %copy.127), calls=%async_computation | async-start | bytes 1310720 | tf_op jit(solution)/shard_map/all_to_all | solution.py:176
  82.0 0.9 convolution_bitcast_fusion.1
  83.1 10.0 %all-to-all-done = f32[1,5,16,8,256]{4,3,1,0,2:T(8,128)S(1)} async-done(((f32[1,5,16,8,256]{4,3,1,0,2:T(8,128)}), f32[1,5,16,8,256]{4,3,1,0,2:T(8,128)S(1)}, u32[]{:S(2)}, u32[]{:S(2)}) %all-to-all-start) | async-done | bytes 655392 | tf_op jit(solution)/shard_map/all_to_all | solution.py:176
  93.5 0.9 fusion.2
  94.4 3.6 %collective-permute-start.2 = (f32[8,2,5,1,3,256]{5,0,4,2,1,3:T(8,128)S(1)}, f32[8,2,5,1,3,256]{5,0,4,2,1,3:T(8,128)S(1)}, u32[]{:S(2)}, u32[]{:S(2)}) collective-permute-start(f32[8,2,5,1,3,256]{5,0,4,2,1,3:T(8,128)S(1)} %get-tuple-element.81), channel_id=1, source_target_pairs={{0,1},{1,2},{2,3},{3,4},{4,5},{5,6},{6,7},{7,8},{8,9},{9,10},{10,1... | collective-permute-start | bytes 737288 | tf_op jit(solution)/shard_map/ppermute | solution.py:28
  98.0 4.7 %collective-permute-start.3 = (f32[8,2,5,1,3,256]{5,0,4,2,1,3:T(8,128)S(1)}, f32[8,2,5,1,3,256]{5,0,4,2,1,3:T(8,128)S(1)}, u32[]{:S(2)}, u32[]{:S(2)}) collective-permute-start(f32[8,2,5,1,3,256]{5,0,4,2,1,3:T(8,128)S(1)} %get-tuple-element.82), channel_id=1, source_target_pairs={{1,0},{2,1},{3,2},{4,3},{5,4},{6,5},{7,6},{8,7},{9,8},{10,9},{11,1... | collective-permute-start | bytes 737288 | tf_op jit(solution)/shard_map/ppermute | solution.py:30
  102.7 6.7 %collective-permute-done.2 = f32[8,2,5,1,3,256]{5,0,4,2,1,3:T(8,128)S(1)} collective-permute-done((f32[8,2,5,1,3,256]{5,0,4,2,1,3:T(8,128)S(1)}, f32[8,2,5,1,3,256]{5,0,4,2,1,3:T(8,128)S(1)}, u32[]{:S(2)}, u32[]{:S(2)}) %collective-permute-start.2) | collective-permute-done | bytes 245792 | tf_op jit(solution)/shard_map/ppermute | solution.py:28
  109.4 7.1 %collective-permute-done.3 = f32[8,2,5,1,3,256]{5,0,4,2,1,3:T(8,128)S(1)} collective-permute-done((f32[8,2,5,1,3,256]{5,0,4,2,1,3:T(8,128)S(1)}, f32[8,2,5,1,3,256]{5,0,4,2,1,3:T(8,128)S(1)}, u32[]{:S(2)}, u32[]{:S(2)}) %collective-permute-start.3) | collective-permute-done | bytes 245792 | tf_op jit(solution)/shard_map/ppermute | solution.py:30
  120.2 0.8 convolution_bitcast_fusion
  121.4 16.3 %all_to_all.38 = f32[16,5,1,8,256]{4,3,1,2,0:T(8,128)S(1)} all-to-all(f32[16,5,1,8,256]{4,3,1,2,0:T(8,128)S(1)} %copy.148), channel_id=1, replica_groups=mesh['inst'=16,'blk'=32] {'inst'}, dimensions={0} | all-to-all | bytes 1310720 | tf_op jit(solution)/shard_map/all_to_all | solution.py:200
  137.6 0.9 copy.149
  (256 shorter events, 21.3 us)
Async XLA Ops:
  0.0 14.0 %copy-start = (f32[1,5,16,8,256]{4,3,2,1,0:T(8,128)S(1)}, f32[1,5,16,8,256]{4,3,2,1,0:T(8,128)}, u32[]{:S(2)}) copy-start(f32[1,5,16,8,256]{4,3,2,1,0:T(8,128)} %param.2) | copy-start | bytes 1966084
  1.5 28.6 %collective-permute-start = (f32[1,5,16,4,256]{4,3,2,1,0:T(4,128)S(1)}, f32[1,5,16,4,256]{4,3,2,1,0:T(4,128)S(1)}, u32[]{:S(2)}, u32[]{:S(2)}) collective-permute-start(f32[1,5,16,4,256]{4,3,2,1,0:T(4,128)S(1)} %get-tuple-element.83), channel_id=1, source_target_pairs={{0,1},{1,2},{2,3},{3,4},{4,5},{5,6},{6,7},{7,8},{8,9},{9,10},{10,1... | collective-permute-start | bytes 983048 | tf_op jit(solution)/shard_map/ppermute | solution.py:28
  7.3 22.8 %collective-permute-start.1 = (f32[1,5,16,4,256]{4,3,2,1,0:T(4,128)S(1)}, f32[1,5,16,4,256]{4,3,2,1,0:T(4,128)S(1)}, u32[]{:S(2)}, u32[]{:S(2)}) collective-permute-start(f32[1,5,16,4,256]{4,3,2,1,0:T(4,128)S(1)} %get-tuple-element.84), channel_id=1, source_target_pairs={{1,0},{2,1},{3,2},{4,3},{5,4},{6,5},{7,6},{8,7},{9,8},{10,9},{11,1... | collective-permute-start | bytes 983048 | tf_op jit(solution)/shard_map/ppermute | solution.py:30
  23.9 51.2 %all-to-all-start.1 = ((f32[16,1,5,1,8,256]{5,4,2,3,1,0:T(8,128)}), f32[16,1,5,1,8,256]{5,4,2,3,1,0:T(8,128)S(1)}, u32[]{:S(2)}, u32[]{:S(2)}) async-start(f32[16,1,5,1,8,256]{5,4,2,3,1,0:T(8,128)} %constant_dynamic-update-slice_fusion), calls=%async_computation.1 | async-start | bytes 1310720 | tf_op jit(solution)/shard_map/all_to_all | solution.py:17
  46.8 1.2 copy-start.30
  47.9 1.8 %copy-start.6 = (f32[1,17,8,256]{3,2,1,0:T(8,128)}, f32[1,17,8,256]{3,2,1,0:T(8,128)S(1)}, u32[]{:S(2)}) copy-start(f32[1,17,8,256]{3,2,1,0:T(8,128)S(1)} %get-tuple-element.18) | copy-start | bytes 417796
  47.9 1.8 %copy-start.8 = (f32[1,17,8,256]{3,2,1,0:T(8,128)}, f32[1,17,8,256]{3,2,1,0:T(8,128)S(1)}, u32[]{:S(2)}) copy-start(f32[1,17,8,256]{3,2,1,0:T(8,128)S(1)} %get-tuple-element.19) | copy-start | bytes 417796
  47.9 1.8 %copy-start.10 = (f32[1,17,8,256]{3,2,1,0:T(8,128)}, f32[1,17,8,256]{3,2,1,0:T(8,128)S(1)}, u32[]{:S(2)}) copy-start(f32[1,17,8,256]{3,2,1,0:T(8,128)S(1)} %get-tuple-element.20) | copy-start | bytes 417796
  47.9 1.8 %copy-start.12 = (f32[1,17,8,256]{3,2,1,0:T(8,128)}, f32[1,17,8,256]{3,2,1,0:T(8,128)S(1)}, u32[]{:S(2)}) copy-start(f32[1,17,8,256]{3,2,1,0:T(8,128)S(1)} %get-tuple-element.21) | copy-start | bytes 417796
  53.9 0.6 copy-start.22
  54.5 0.6 copy-start.24
  56.6 0.6 copy-start.26
  57.2 0.6 copy-start.28
  60.3 0.6 copy-start.20
  64.5 2.1 %copy-start.14 = (f32[1,16,8,258]{3,2,1,0:T(8,128)S(1)}, f32[1,16,8,258]{3,2,1,0:T(8,128)}, u32[]{:S(2)}) copy-start(f32[1,16,8,258]{3,2,1,0:T(8,128)} %minimum_add_fusion.24) | copy-start | bytes 396292
  64.5 2.1 %copy-start.15 = (f32[1,16,8,258]{3,2,1,0:T(8,128)S(1)}, f32[1,16,8,258]{3,2,1,0:T(8,128)}, u32[]{:S(2)}) copy-start(f32[1,16,8,258]{3,2,1,0:T(8,128)} %minimum_add_fusion.23) | copy-start | bytes 396292
  64.5 2.1 %copy-start.21 = (f32[1,16,8,2]{3,2,1,0:T(8,128)S(1)}, f32[1,16,8,2]{3,2,1,0:T(8,128)}, u32[]{:S(2)}) copy-start(f32[1,16,8,2]{3,2,1,0:T(8,128)} %copy-done.20) | copy-start | bytes 3076
  64.5 2.1 %copy-start.23 = (f32[1,16,8,2]{3,2,1,0:T(8,128)S(1)}, f32[1,16,8,2]{3,2,1,0:T(8,128)}, u32[]{:S(2)}) copy-start(f32[1,16,8,2]{3,2,1,0:T(8,128)} %copy-done.22) | copy-start | bytes 3076
  64.5 2.1 %copy-start.25 = (f32[1,16,8,2]{3,2,1,0:T(8,128)S(1)}, f32[1,16,8,2]{3,2,1,0:T(8,128)}, u32[]{:S(2)}) copy-start(f32[1,16,8,2]{3,2,1,0:T(8,128)} %copy-done.24) | copy-start | bytes 3076
  64.6 2.1 %copy-start.27 = (f32[1,16,8,2]{3,2,1,0:T(8,128)S(1)}, f32[1,16,8,2]{3,2,1,0:T(8,128)}, u32[]{:S(2)}) copy-start(f32[1,16,8,2]{3,2,1,0:T(8,128)} %copy-done.26) | copy-start | bytes 3076
  64.6 2.1 %copy-start.29 = (f32[1,16,8,2]{3,2,1,0:T(8,128)S(1)}, f32[1,16,8,2]{3,2,1,0:T(8,128)}, u32[]{:S(2)}) copy-start(f32[1,16,8,2]{3,2,1,0:T(8,128)} %copy-done.28) | copy-start | bytes 3076
  67.9 1.0 copy-start.5
  67.9 1.0 copy-start.4
  67.9 1.1 copy-start.3
  68.9 1.0 copy-start.2
  68.9 1.0 copy-start.1
  70.9 0.9 copy-start.19
  70.9 1.0 copy-start.18
  72.0 0.9 copy-start.17
  72.0 1.0 copy-start.7
  72.0 1.0 copy-start.9
  72.1 1.1 copy-start.11
  72.1 1.1 copy-start.13
  72.1 1.1 copy-start.31
  73.2 0.9 copy-start.16
  74.2 7.7 %copy-start.32 = (s32[7]{0:T(128)S(1)}, s32[7]{0:T(128)}, u32[]{:S(2)}) copy-start(s32[7]{0:T(128)} %param.3) | copy-start | bytes 88
  75.2 18.0 %all-to-all-start = ((f32[1,5,16,8,256]{4,3,1,0,2:T(8,128)}), f32[1,5,16,8,256]{4,3,1,0,2:T(8,128)S(1)}, u32[]{:S(2)}, u32[]{:S(2)}) async-start(f32[1,5,16,8,256]{4,3,1,0,2:T(8,128)} %copy.127), calls=%async_computation | async-start | bytes 1310720 | tf_op jit(solution)/shard_map/all_to_all | solution.py:176
  94.4 15.0 %collective-permute-start.2 = (f32[8,2,5,1,3,256]{5,0,4,2,1,3:T(8,128)S(1)}, f32[8,2,5,1,3,256]{5,0,4,2,1,3:T(8,128)S(1)}, u32[]{:S(2)}, u32[]{:S(2)}) collective-permute-start(f32[8,2,5,1,3,256]{5,0,4,2,1,3:T(8,128)S(1)} %get-tuple-element.81), channel_id=1, source_target_pairs={{0,1},{1,2},{2,3},{3,4},{4,5},{5,6},{6,7},{7,8},{8,9},{9,10},{10,1... | collective-permute-start | bytes 737288 | tf_op jit(solution)/shard_map/ppermute | solution.py:28
  98.0 18.5 %collective-permute-start.3 = (f32[8,2,5,1,3,256]{5,0,4,2,1,3:T(8,128)S(1)}, f32[8,2,5,1,3,256]{5,0,4,2,1,3:T(8,128)S(1)}, u32[]{:S(2)}, u32[]{:S(2)}) collective-permute-start(f32[8,2,5,1,3,256]{5,0,4,2,1,3:T(8,128)S(1)} %get-tuple-element.82), channel_id=1, source_target_pairs={{1,0},{2,1},{3,2},{4,3},{5,4},{6,5},{7,6},{8,7},{9,8},{10,9},{11,1... | collective-permute-start | bytes 737288 | tf_op jit(solution)/shard_map/ppermute | solution.py:30
